TPU v7x, 128 devices: a whole 4x4x4 slice. The times are simulated.
128 devices in a mesh: mrow: 4 (over x), mcol: 4 (over y), sub: 8 (over z, core).
Axes of the slice: x: 4, y: 4, z: 4, core: 2. Of those that a mesh axis runs over, the one named last changes fastest.
Arguments:
- deflation: bfloat16 [64, 64, 256, 1024], P(None, 'sub', 'mcol', 'mrow'), may hold values from -0.13258252 to 0.13258252
- reaction: float32 [64, 256, 1024], P('sub', 'mcol', 'mrow'), may hold values from 0.005 to 0.16
- vector_counts: int32 [128], P(('mrow', 'mcol', 'sub')), may hold values from 32 to 64
Outputs:
- coarse_factor: float32 [8192, 8192], P(('mrow', 'mcol', 'sub'))
All inputs are finite; a program needn't handle non-finite values.
Results may differ from a plain program's by a relative error of at most 0.0003.
Values may be sent and summed in bfloat16 or wider, within the bound.
A program may use at most 192 MiB of HBM per device.

v0:
```python
import jax
import jax.numpy as jnp
import numpy as np
from jax import lax
from jax.sharding import PartitionSpec as P

PANEL = 256
PANELS = 2


def padded_2(cells, sides, width):
    for axis, dim in sides:
        count = lax.axis_size(axis)
        ends = count - 1
        head = lax.slice_in_dim(cells, 0, width, axis=dim)
        tail = lax.slice_in_dim(cells, cells.shape[dim] - width, cells.shape[dim], axis=dim)
        cells = jnp.concatenate(
            [
                lax.ppermute(tail, axis, [(i, (i + 1) % count) for i in range(ends)]),
                cells,
                lax.ppermute(head, axis, [((i + 1) % count, i) for i in range(ends)]),
            ],
            axis=dim,
        )
    return cells


def apply_local(block, weight):
    padded = jnp.pad(block, ((0, 0), (1, 1), (1, 1), (1, 1)))
    beside = padded[:, 2:, 1:-1, 1:-1].astype(jnp.float32) + padded[:, :-2, 1:-1, 1:-1].astype(
        jnp.float32
    )
    beside = (
        beside
        + padded[:, 1:-1, 2:, 1:-1].astype(jnp.float32)
        + padded[:, 1:-1, :-2, 1:-1].astype(jnp.float32)
    )
    beside = (
        beside
        + padded[:, 1:-1, 1:-1, 2:].astype(jnp.float32)
        + padded[:, 1:-1, 1:-1, :-2].astype(jnp.float32)
    )
    return ((6.0 + weight)[None] * block.astype(jnp.float32) - beside).astype(jnp.bfloat16)


def inner_products(left_side, right_side):
    vectors = left_side.shape[0]
    return lax.dot_general(
        left_side.reshape(vectors, -1),
        right_side.reshape(vectors, -1),
        (((1,), (1,)), ((), ())),
        preferred_element_type=jnp.float32,
    )


def couple(own_face, other_face):
    return -inner_products(own_face, other_face)


def place(row_block, block, block_id):
    width = block.shape[0]
    current = lax.dynamic_slice_in_dim(row_block, block_id * width, width, 1)
    return lax.dynamic_update_slice_in_dim(row_block, current + block, block_id * width, 1)


def outer_rows(left_rows, right_rows):
    return lax.dot_general(
        left_rows,
        right_rows,
        (((1,), (1,)), ((), ())),
        precision=lax.Precision.HIGHEST,
        preferred_element_type=jnp.float32,
    )


def panel_blocks(sub_count, col_count, row_count, vectors, panel_width, panel_total):
    total_blocks = sub_count * col_count * row_count
    block_ids = np.arange(total_blocks)
    pattern = np.eye(total_blocks, dtype=bool)
    sub_pos = block_ids % sub_count
    col_pos = block_ids // sub_count % col_count
    row_pos = block_ids // (sub_count * col_count)
    for stride, usable in (
        (1, sub_pos != sub_count - 1),
        (sub_count, col_pos != col_count - 1),
        (sub_count * col_count, row_pos != row_count - 1),
    ):
        source = block_ids[usable]
        pattern[source, source + stride] = True
        pattern[source + stride, source] = True
    listed = []
    for panel_id in range(panel_total):
        first_col = panel_id * panel_width
        first_block = first_col // vectors
        last_block = (first_col + panel_width - 1) // vectors
        touched = pattern[:, first_block : last_block + 1].any(axis=1) & (
            (block_ids + 1) * vectors > first_col
        )
        listed.append(block_ids[touched])
        pattern = pattern | touched[:, None] & touched[None, :]
    return listed


def shards(deflation, reaction, vector_counts):
    vectors = deflation.shape[0]
    sub_count = lax.axis_size("sub")
    col_count = lax.axis_size("mcol")
    row_count = lax.axis_size("mrow")
    order_total = vectors * sub_count * col_count * row_count
    position = lax.axis_index(("mrow", "mcol", "sub"))
    live_mask = lax.iota(jnp.int32, vectors) < vector_counts[0]
    masked = deflation * live_mask.astype(jnp.bfloat16)[:, None, None, None]
    applied = apply_local(masked, reaction)
    gram_block = inner_products(masked, applied)
    diagonal_block = 0.5 * (gram_block + gram_block.T) + jnp.diag(
        1.0 - live_mask.astype(jnp.float32)
    )
    extended = padded_2(masked, (("mrow", 3), ("mcol", 2), ("sub", 1)), 1)
    low_x = couple(masked[:, 0], extended[:, 0, 1:-1, 1:-1])
    high_x = couple(masked[:, -1], extended[:, -1, 1:-1, 1:-1])
    low_y = couple(masked[:, :, 0], extended[:, 1:-1, 0, 1:-1])
    high_y = couple(masked[:, :, -1], extended[:, 1:-1, -1, 1:-1])
    low_z = couple(masked[:, :, :, 0], extended[:, 1:-1, 1:-1, 0])
    high_z = couple(masked[:, :, :, -1], extended[:, 1:-1, 1:-1, -1])
    row_block = place(jnp.zeros((vectors, order_total), jnp.float32), diagonal_block, position)
    plane_step = sub_count * col_count
    for offset, block in (
        (-1, low_x),
        (1, high_x),
        (-sub_count, low_y),
        (sub_count, high_y),
        (-plane_step, low_z),
        (plane_step, high_z),
    ):
        row_block = place(row_block, block, position + offset)
    rows_global = position * vectors + lax.iota(jnp.int32, vectors)
    blocks_listed = panel_blocks(sub_count, col_count, row_count, vectors, PANEL, PANELS)
    factors = []
    for panel_id in range(PANELS):
        first_col = panel_id * PANEL
        columns = row_block[:, first_col : first_col + PANEL]
        chosen = blocks_listed[panel_id]
        count_active = chosen.shape[0]
        row_ids = (
            (chosen[:, None] * vectors + np.arange(vectors)[None, :]).reshape(-1).astype(np.int32)
        )
        slot_mask = (jnp.asarray(chosen.astype(np.int32)) == position).astype(jnp.float32)
        contribution = slot_mask[:, None, None] * columns[None]
        compact = lax.psum(contribution, ("mrow", "mcol", "sub"))
        stacked = compact.reshape(count_active * vectors, PANEL)
        pivot_start = int(np.searchsorted(row_ids, first_col))
        pivot_factor = jnp.linalg.cholesky(stacked[pivot_start : pivot_start + PANEL])
        active_rows = jax.scipy.linalg.solve_triangular(pivot_factor, stacked.T, lower=True).T
        active_rows = jnp.where(jnp.asarray(row_ids >= first_col)[:, None], active_rows, 0.0)
        own_rows = jax.scipy.linalg.solve_triangular(pivot_factor, columns.T, lower=True).T
        own_rows = jnp.where((rows_global >= first_col)[:, None], own_rows, 0.0)
        product = outer_rows(own_rows, active_rows)
        update = (
            jnp.zeros((vectors, order_total), jnp.float32).at[:, jnp.asarray(row_ids)].set(product)
        )
        row_block = row_block - update
        factors.append(own_rows)
    finished = PANELS * PANEL
    trailing = jnp.where((rows_global >= finished)[:, None], row_block[:, finished:], 0.0)
    return jnp.concatenate(factors + [trailing], axis=1)


def solution(mesh):
    return jax.shard_map(
        shards,
        mesh=mesh,
        in_specs=(
            P(None, "sub", "mcol", "mrow"),
            P("sub", "mcol", "mrow"),
            P(("mrow", "mcol", "sub")),
        ),
        out_specs=P(("mrow", "mcol", "sub"), None),
        check_vma=False,
    )
```

profile of v0, /device:TPU:2, one launch (start us, length us, event | category | flops | bytes accessed | tf_op | source)
XLA Modules:
  0.0 687.3 jit_solution(12656876850650809079)
XLA Ops:
  7.2 14.7 %copy_multiply_fusion = bf16[64,8,64,256]{3,0,2,1:T(8,128)(2,1)S(1)} fusion(bf16[64,8,64,256]{3,2,1,0:T(8,128)(2,1)} %param.12, bf16[64]{0:T(256)(128)(2,1)S(1)} %compare_convert_fusion.3), kind=kLoop, calls=%fused_computation.14 | loop fusion | flops 8388608 | bytes 33554560 | tf_op jit(solution)/shard_map/mul | solution.py:112
  22.0 8.7 %fusion.77 = (bf16[64,8,64,1]{3,0,2,1:T(8,128)(2,1)}, bf16[64,8,64,1]{3,0,2,1:T(8,128)(2,1)}) fusion(bf16[64,8,64,256]{3,0,2,1:T(8,128)(2,1)S(1)} %copy_multiply_fusion), kind=kLoop, calls=%fused_computation.161 | loop fusion | bytes 262144 | tf_op jit(solution)/shard_map/slice | solution.py:16
  30.7 2.0 copy-done
  32.7 9.3 %copy.46 = bf16[64,8,64,1]{2,1,3,0:T(8,128)(2,1)S(1)} copy(bf16[64,8,64,1]{3,0,2,1:T(8,128)(2,1)} %get-tuple-element.63) | data formatting | bytes 131072 | tf_op jit(solution)/shard_map/slice | solution.py:16
  42.0 3.4 collective-permute-start
  45.4 9.3 %copy.47 = bf16[64,8,64,1]{2,1,3,0:T(8,128)(2,1)S(1)} copy(bf16[64,8,64,1]{3,0,2,1:T(8,128)(2,1)} %get-tuple-element.64) | data formatting | bytes 131072 | tf_op jit(solution)/shard_map/slice | solution.py:15
  54.7 2.4 collective-permute-start.1
  57.1 7.0 %copy.48 = bf16[64,8,64,1]{3,0,2,1:T(8,128)(2,1)} copy(bf16[64,8,64,1]{2,1,3,0:T(8,128)(2,1)S(1)} %collective-permute-done) | data formatting | bytes 131072 | tf_op jit(solution)/shard_map/ppermute | solution.py:19
  64.2 7.1 %copy.49 = bf16[64,8,64,1]{3,0,2,1:T(8,128)(2,1)} copy(bf16[64,8,64,1]{2,1,3,0:T(8,128)(2,1)S(1)} %collective-permute-done.1) | data formatting | bytes 131072 | tf_op jit(solution)/shard_map/ppermute | solution.py:21
  71.2 1.8 pad_maximum_fusion.8
  73.1 3.8 collective-permute-start.2
  78.2 6.4 collective-permute-done.2
  84.6 4.1 collective-permute-done.3
  88.8 8.0 %pad_maximum_fusion = (bf16[64,1,66,258]{3,0,2,1:T(8,128)(2,1)}, bf16[64,1,66,258]{3,0,2,1:T(8,128)(2,1)}) fusion(bf16[64,8,1,258]{3,0,2,1:T(8,128)(2,1)S(1)} %collective-permute-done.3, bf16[64,8,1,258]{3,0,2,1:T(8,128)(2,1)S(1)} %collective-permute-done.2, bf16[64,8,64,1]{3,0,2,1:T(8,128)(2,1)S(1)} %copy-done.1, bf16[64,8,64,256]{3,0,2,1:T(8,128)(2,1)} %copy-done, ...), kind=kLoop, calls=%fused_computation.16 | loop fusion | flops 21795840 | bytes 21795840 | tf_op jit(solution)/shard_map/concatenate | solution.py:17
  96.8 3.1 collective-permute-start.4
  100.0 45.1 %subtract_convert_fusion.6 = bf16[64,8,64,256]{3,0,2,1:T(8,128)(2,1)} fusion(bf16[64,8,64,256]{3,0,2,1:T(8,128)(2,1)} %copy-done, f32[8,64,256]{2,1,0:T(8,128)S(1)} %broadcast_add_fusion), kind=kLoop, calls=%fused_computation.12.clone.clone.clone.clone.1 | loop fusion | flops 125829120 | bytes 34078720 | tf_op jit(solution)/shard_map/dot_general | solution.py:48
  145.1 10.8 %copy.69 = bf16[64,8,64,1]{2,0,1,3:T(8,128)(2,1)S(1)} copy(bf16[64,8,64,1]{3,0,2,1:T(8,128)(2,1)} %get-tuple-element.63) | data formatting | bytes 131072 | tf_op jit(solution)/shard_map/reshape.48
  155.9 10.8 %copy.68 = bf16[64,8,64,1]{2,0,1,3:T(8,128)(2,1)S(1)} copy(bf16[64,8,64,1]{3,0,2,1:T(8,128)(2,1)} %get-tuple-element.64) | data formatting | bytes 131072 | tf_op jit(solution)/shard_map/reshape.46
  166.7 1.4 collective-permute-start.5
  168.1 12.9 %fusion.15 = f32[64,64]{1,0:T(8,128)S(1)} fusion(bf16[64,8,64,256]{3,0,2,1:T(8,128)(2,1)} %copy-done, bf16[64,8,64,256]{3,0,2,1:T(8,128)(2,1)} %subtract_convert_fusion.6), kind=kOutput, calls=%fused_computation.44 | convolution fusion | flops 1073741824 | bytes 33570816 | tf_op jit(solution)/shard_map/dot_general | solution.py:48
  181.8 3.5 fusion.25
  185.9 3.5 dynamic-slice_add_fusion.1
  196.3 167.8 %all-reduce.5.cloned.1.call-done = f32[13,64,256]{2,1,0:T(8,128)} async-done(((f32[13,64,256]{2,1,0:T(8,128)}), f32[13,64,256]{2,1,0:T(8,128)}) %all-reduce.5.cloned.1.call-update) | async-done | bytes 851984 | tf_op jit(solution)/shard_map/psum | solution.py:149
  366.1 11.7 %cholesky.130 = f32[128,128]{1,0:T(8,128)S(1)} custom-call(f32[128,128]{1,0:T(8,128)S(1)} %cholesky.194), custom_call_target="Cholesky" | custom-call | tf_op jit(solution)/shard_map/jit(cholesky)/cholesky | solution.py:152
  377.8 9.8 %custom-call.23 = f32[1,128,128]{1,2,0:T(8,128)S(1)} custom-call(f32[1,128,128]{2,1,0:T(8,128)S(1)} %get-tuple-element.76), custom_call_target="InvertDiagBlocksLowerTriangular" | custom-call | tf_op jit(solution)/shard_map/jit(cholesky)/cholesky | solution.py:152
  389.8 11.7 %cholesky.147 = f32[128,128]{1,0:T(8,128)S(1)} custom-call(f32[128,128]{1,0:T(8,128)S(1)} %convolution_subtract_fusion.3), custom_call_target="Cholesky" | custom-call | tf_op jit(solution)/shard_map/jit(cholesky)/cholesky | solution.py:152
  403.7 4.1 while.6
  404.5 1.4 bitcast_dynamic-update-slice_fusion.4
  406.5 1.4 bitcast_dynamic-update-slice_fusion.4
  407.8 19.7 %custom-call.24 = f32[2,128,128]{1,2,0:T(8,128)S(1)} custom-call(f32[2,128,128]{2,1,0:T(8,128)S(1)} %get-tuple-element.37), custom_call_target="InvertDiagBlocksLowerTriangular" | custom-call | tf_op jit(solution)/shard_map/jit(_solve_triangular)/triangular_solve | solution.py:155
  430.6 6.4 scatter_custom_fusion
  437.0 4.0 copy.59
  441.0 1.8 sub.22
  442.8 1.3 copy-done.2
  445.5 147.8 %all-reduce.7.cloned.1.call-done = f32[20,64,256]{2,1,0:T(8,128)} async-done(((f32[20,64,256]{2,1,0:T(8,128)}), f32[20,64,256]{2,1,0:T(8,128)}) %all-reduce.7.cloned.1.call-update) | async-done | bytes 1310736 | tf_op jit(solution)/shard_map/psum | solution.py:149
  594.5 11.7 %cholesky.164 = f32[128,128]{1,0:T(8,128)S(1)} custom-call(f32[128,128]{1,0:T(8,128)S(1)} %cholesky.197), custom_call_target="Cholesky" | custom-call | tf_op jit(solution)/shard_map/jit(cholesky)/cholesky | solution.py:152
  606.9 9.8 %custom-call.25 = f32[1,128,128]{1,2,0:T(8,128)S(1)} custom-call(f32[1,128,128]{2,1,0:T(8,128)S(1)} %get-tuple-element.72), custom_call_target="InvertDiagBlocksLowerTriangular" | custom-call | tf_op jit(solution)/shard_map/jit(cholesky)/cholesky | solution.py:152
  617.2 11.7 %cholesky.181 = f32[128,128]{1,0:T(8,128)S(1)} custom-call(f32[128,128]{1,0:T(8,128)S(1)} %convolution_subtract_fusion.2), custom_call_target="Cholesky" | custom-call | tf_op jit(solution)/shard_map/jit(cholesky)/cholesky | solution.py:152
  630.9 3.8 while.7
  631.5 1.3 bitcast_dynamic-update-slice_fusion.5
  633.5 1.3 bitcast_dynamic-update-slice_fusion.5
  634.8 19.9 %custom-call.26 = f32[2,128,128]{1,2,0:T(8,128)S(1)} custom-call(f32[2,128,128]{2,1,0:T(8,128)S(1)} %get-tuple-element.38), custom_call_target="InvertDiagBlocksLowerTriangular" | custom-call | tf_op jit(solution)/shard_map/jit(_solve_triangular)/triangular_solve | solution.py:155
  658.0 2.2 fusion.9
  660.3 8.4 %scatter_custom_fusion.1 = f32[64,8192]{0,1:T(8,128)} fusion(s32[1280]{0:T(1024)} %constant.206, f32[1280,64]{1,0:T(8,128)S(1)} %fusion.9, f32[]{:T(128)} %constant.128.clone.1), kind=kCustom, calls=%fused_computation.29 | custom fusion | bytes 2097664 | tf_op jit(solution)/shard_map/scatter | solution.py:159
  668.7 4.2 slice.223
  672.9 3.9 copy.76
  676.8 1.8 fusion.8
  678.6 1.5 pad_maximum_fusion.5
  (103 shorter events, 27.5 us)
Async XLA Ops:
  6.5 357.6 %all-reduce.5.cloned.1.call-start = ((), (), s32[]{:S(2)}) async-start(), calls=%async_computation | async-start | bytes 1703936 | tf_op jit(solution)/shard_map/psum | solution.py:149
  21.9 10.7 %copy-start = (bf16[64,8,64,256]{3,0,2,1:T(8,128)(2,1)}, bf16[64,8,64,256]{3,0,2,1:T(8,128)(2,1)S(1)}, u32[]{:S(2)}) copy-start(bf16[64,8,64,256]{3,0,2,1:T(8,128)(2,1)S(1)} %copy_multiply_fusion) | copy-start | bytes 50331652
  42.0 15.2 %collective-permute-start = (bf16[64,8,64,1]{2,1,3,0:T(8,128)(2,1)S(1)}, bf16[64,8,64,1]{2,1,3,0:T(8,128)(2,1)S(1)}, u32[]{:S(2)}, u32[]{:S(2)}) collective-permute-start(bf16[64,8,64,1]{2,1,3,0:T(8,128)(2,1)S(1)} %copy.46), channel_id=1, source_target_pairs={{0,32},{32,64},{64,96},{1,33},{33,65},{65,97},{2,34},{34,66},{66,9... | collective-permute-start | bytes 196616 | tf_op jit(solution)/shard_map/ppermute | solution.py:19
  54.7 9.5 %collective-permute-start.1 = (bf16[64,8,64,1]{2,1,3,0:T(8,128)(2,1)S(1)}, bf16[64,8,64,1]{2,1,3,0:T(8,128)(2,1)S(1)}, u32[]{:S(2)}, u32[]{:S(2)}) collective-permute-start(bf16[64,8,64,1]{2,1,3,0:T(8,128)(2,1)S(1)} %copy.47), channel_id=1, source_target_pairs={{32,0},{64,32},{96,64},{33,1},{65,33},{97,65},{34,2},{66,34},{98,6... | collective-permute-start | bytes 196616 | tf_op jit(solution)/shard_map/ppermute | solution.py:21
  71.2 6.9 %copy-start.7 = (f32[8,64,256]{2,1,0:T(8,128)S(1)}, f32[8,64,256]{2,1,0:T(8,128)}, u32[]{:S(2)}) copy-start(f32[8,64,256]{2,1,0:T(8,128)} %param.13) | copy-start | bytes 1572868
  71.2 17.5 %copy-start.1 = (bf16[64,8,64,1]{3,0,2,1:T(8,128)(2,1)S(1)}, bf16[64,8,64,1]{3,0,2,1:T(8,128)(2,1)}, u32[]{:S(2)}) copy-start(bf16[64,8,64,1]{3,0,2,1:T(8,128)(2,1)} %copy.49) | copy-start | bytes 196612
  73.1 11.5 %collective-permute-start.2 = (bf16[64,8,1,258]{3,0,2,1:T(8,128)(2,1)S(1)}, bf16[64,8,1,258]{3,0,2,1:T(8,128)(2,1)S(1)}, u32[]{:S(2)}, u32[]{:S(2)}) collective-permute-start(bf16[64,8,1,258]{3,0,2,1:T(8,128)(2,1)S(1)} %get-tuple-element.61), channel_id=1, source_target_pairs={{0,8},{8,16},{16,24},{1,9},{9,17},{17,25},{2,10},{10,18},{18,26},{... | collective-permute-start | bytes 792584 | tf_op jit(solution)/shard_map/ppermute | solution.py:19
  76.9 11.9 %collective-permute-start.3 = (bf16[64,8,1,258]{3,0,2,1:T(8,128)(2,1)S(1)}, bf16[64,8,1,258]{3,0,2,1:T(8,128)(2,1)S(1)}, u32[]{:S(2)}, u32[]{:S(2)}) collective-permute-start(bf16[64,8,1,258]{3,0,2,1:T(8,128)(2,1)S(1)} %get-tuple-element.62), channel_id=1, source_target_pairs={{8,0},{16,8},{24,16},{9,1},{17,9},{25,17},{10,2},{18,10},{26,18},{... | collective-permute-start | bytes 792584 | tf_op jit(solution)/shard_map/ppermute | solution.py:21
  96.8 85.0 %collective-permute-start.4 = (bf16[64,1,66,258]{3,0,2,1:T(8,128)(2,1)}, bf16[64,1,66,258]{3,0,2,1:T(8,128)(2,1)}, u32[]{:S(2)}, u32[]{:S(2)}) collective-permute-start(bf16[64,1,66,258]{3,0,2,1:T(8,128)(2,1)} %get-tuple-element.60), channel_id=1, source_target_pairs={{0,1},{1,2},{2,3},{3,4},{4,5},{5,6},{6,7},{8,9},{9,10},{10,11},{11... | collective-permute-start | bytes 6538760 | tf_op jit(solution)/shard_map/ppermute | solution.py:19
  166.7 15.1 %copy-start.9 = (s32[13]{0:T(128)S(1)}, s32[13]{0:T(128)}, u32[]{:S(2)}) copy-start(s32[13]{0:T(128)} %constant.141.clone) | copy-start | bytes 160
  166.7 19.2 %collective-permute-start.5 = (bf16[64,1,66,258]{3,0,2,1:T(8,128)(2,1)}, bf16[64,1,66,258]{3,0,2,1:T(8,128)(2,1)}, u32[]{:S(2)}, u32[]{:S(2)}) collective-permute-start(bf16[64,1,66,258]{3,0,2,1:T(8,128)(2,1)} %get-tuple-element.59), channel_id=1, source_target_pairs={{1,0},{2,1},{3,2},{4,3},{5,4},{6,5},{7,6},{9,8},{10,9},{11,10},{12... | collective-permute-start | bytes 6538760 | tf_op jit(solution)/shard_map/ppermute | solution.py:21
  185.9 10.4 %copy-start.8 = (s32[20]{0:T(128)S(1)}, s32[20]{0:T(128)}, u32[]{:S(2)}) copy-start(s32[20]{0:T(128)} %constant.144.clone) | copy-start | bytes 244
  195.8 397.4 %all-reduce.7.cloned.1.call-start = ((), (), s32[]{:S(2)}) async-start(), calls=%async_computation.1 | async-start | bytes 2621440 | tf_op jit(solution)/shard_map/psum | solution.py:149
  364.2 64.0 %copy-start.5 = (f32[13,64,256]{2,1,0:T(8,128)S(1)}, f32[13,64,256]{2,1,0:T(8,128)}, u32[]{:S(2)}) copy-start(f32[13,64,256]{2,1,0:T(8,128)} %all-reduce.5.cloned.1.call-done) | copy-start | bytes 2555908
  365.4 0.7 copy-start.6
  442.8 1.3 copy-start.2
  593.2 62.1 %copy-start.4 = (f32[20,64,256]{2,1,0:T(8,128)S(1)}, f32[20,64,256]{2,1,0:T(8,128)}, u32[]{:S(2)}) copy-start(f32[20,64,256]{2,1,0:T(8,128)} %all-reduce.7.cloned.1.call-done) | copy-start | bytes 3932164
  672.9 3.9 copy-start.3
Sparse Core Ops, SparseCore 0:
  195.9 168.1 all-reduce.4
  445.5 147.7 all-reduce.6
where the time goes:
time: 696 us; the launch traced here: 687 us
  waiting for transfers between devices  326 us (47%)
  other arithmetic  186 us (27%)
  local copies, waits for them, and re-layouts  108 us (16%)
  matrix products  33.3 us (5%)
  between operations  17.6 us (3%)
  starting transfers between devices  15.9 us (2%)
    psum x2, waiting for transfers between devices, shards(): compact = lax.psum(contribution, ('mrow', 'mcol', 'sub'))  316 us
    another operation x13, other arithmetic, shards(): pivot_factor = jnp.linalg.cholesky(stacked[pivot_start:pivot_start + PANEL])  68.6 us
    dot_general x1, other arithmetic, inner_products(): lax.dot_general(left_side.reshape(vectors, -1), right_side.reshape(vector...  45.1 us
    another operation x5, other arithmetic, shards(): jax.scipy.linalg.solve_triangular(pivot_factor, columns.T, lower=True)  39.7 us
    dot_general x7, matrix products, inner_products(): lax.dot_general(left_side.reshape(vectors, -1), right_side.reshape(vector...  22.7 us
    another operation x3, local copies, waits for them, and re-layouts  21.7 us
    scatter x3, local copies, waits for them, and re-layouts, shards(): jnp.zeros((vectors, order_total), jnp.float32).at[:, jnp.asarray(row_ids)]  18.8 us
    slice x2, local copies, waits for them, and re-layouts, padded_2(): lax.slice_in_dim(cells, cells.shape[dim] - width, cells.shape[dim], axis=...  18 us
  transfers between devices with their start and end apart: 8, of which 4 were waited for; matrix products, arithmetic and copies ran while one was open for 15% of the time, Pallas kernels for 0%

commit v1 on v0

v1 whole, which is shorter than its diff:
```python
import functools

import jax
import jax.numpy as jnp
from jax import lax
from jax.experimental import pallas as pl
from jax.experimental.pallas import tpu as pltpu
from jax.sharding import PartitionSpec as P

MESH = pl.DeviceIdType.MESH
F32 = jnp.float32
BF16 = jnp.bfloat16
HI = lax.Precision.HIGHEST
K = 64
CX = 8
CY = 64
CZ = 256
ROWS = K * 8
SUB = 8


def dot_nt(a, b, precision=None):
    return lax.dot_general(
        a, b, (((1,), (1,)), ((), ())), precision=precision, preferred_element_type=F32
    )


def dot_nn(a, b, precision=None):
    return lax.dot_general(
        a, b, (((1,), (0,)), ((), ())), precision=precision, preferred_element_type=F32
    )


def dot_tn(a, b, precision=None):
    return lax.dot_general(
        a, b, (((0,), (0,)), ((), ())), precision=precision, preferred_element_type=F32
    )


def iota(shape, axis):
    return lax.broadcasted_iota(jnp.int32, shape, axis)


def fold(product):
    same = (iota(product.shape, 0) & 7) == (iota(product.shape, 1) & 7)
    kept = jnp.where(same, product, 0.0).reshape(K, 8, ROWS).sum(axis=1)
    collect = ((iota((ROWS, K), 0) >> 3) == iota((ROWS, K), 1)).astype(F32)
    return dot_nn(kept, collect, HI)


def assemble_kernel(
    defl,
    react,
    count,
    own_out,
    gathered,
    mbuf,
    left,
    right,
    acc,
    weight,
    zrows,
    ylow,
    yhigh,
    yrecv,
    zhigh,
    zrecv,
    xrecv_low,
    xrecv_high,
    mask_own,
    mask_recv,
    part_send,
    part_recv,
    load_sem,
    mask_send_sem,
    mask_recv_sem,
    face_send_sem,
    face_recv_sem,
    part_send_sem,
    part_recv_sem,
    line_send_sem,
    cross_send_sem,
    line_recv_sem,
):
    mrow = lax.axis_index("mrow")
    mcol = lax.axis_index("mcol")
    sub = lax.axis_index("sub")
    mrows = lax.axis_size("mrow")
    mcols = lax.axis_size("mcol")
    s_next, s_prev = lax.rem(sub + 1, SUB), lax.rem(sub + SUB - 1, SUB)
    j_next, j_prev = lax.rem(mcol + 1, mcols), lax.rem(mcol + mcols - 1, mcols)
    i_next, i_prev = lax.rem(mrow + 1, mrows), lax.rem(mrow + mrows - 1, mrows)

    loads = [
        pltpu.make_async_copy(defl.at[:, x], mbuf.at[x], load_sem.at[x]) for x in range(CX)
    ]
    for load in loads:
        load.start()

    barrier = pltpu.get_barrier_semaphore()
    for step in range(1, SUB):
        pl.semaphore_signal(
            barrier,
            inc=1,
            device_id={"sub": lax.rem(sub + step, SUB)},
            device_id_type=MESH,
        )
    for axis, other in (
        ("mcol", j_next),
        ("mcol", j_prev),
        ("mrow", i_next),
        ("mrow", i_prev),
    ):
        pl.semaphore_signal(barrier, inc=1, device_id={axis: other}, device_id_type=MESH)
    pl.semaphore_wait(barrier, SUB - 1 + 4)

    def remote(src, dst, send, recv, target):
        return pltpu.make_async_remote_copy(
            src_ref=src,
            dst_ref=dst,
            send_sem=send,
            recv_sem=recv,
            device_id=target,
            device_id_type=MESH,
        )

    xface_up = remote(
        defl.at[:, CX - 1, 0 : CY // 2],
        xrecv_low,
        face_send_sem.at[0],
        face_recv_sem.at[0],
        {"sub": s_next},
    )
    xface_down = remote(
        defl.at[:, 0, CY // 2 : CY],
        xrecv_high,
        face_send_sem.at[1],
        face_recv_sem.at[1],
        {"sub": s_prev},
    )
    xface_up.start()
    xface_down.start()

    live = count[0]
    mask_own[...] = (iota((8, 128), 1) < live).astype(F32)
    masks = []
    for slot, target in enumerate(
        (
            {"sub": s_next},
            {"sub": s_prev},
            {"mcol": j_next},
            {"mcol": j_prev},
            {"mrow": i_next},
            {"mrow": i_prev},
        )
    ):
        masks.append(
            remote(
                mask_own,
                mask_recv.at[slot],
                mask_send_sem.at[slot],
                mask_recv_sem.at[slot],
                target,
            )
        )
        masks[-1].start()

    weight[...] = 3.0 + 0.5 * react[...]
    mbuf[CX] = jnp.zeros((K, CY, CZ), BF16)
    acc[...] = jnp.zeros_like(acc)
    part_send[...] = jnp.zeros_like(part_send)
    tail = iota((16, 8 * CZ), 0)
    spot = (tail & 7) * CZ + (tail >> 3) * (CZ - 1)
    left[ROWS : ROWS + 16, :] = (iota((16, 8 * CZ), 1) == spot).astype(F32).astype(BF16)

    def rows_of(value, block):
        return value[:, 8 * block : 8 * block + 8, :].reshape(16, CZ).astype(BF16)

    def plane(x, carry):
        def pair(step, inner):
            first = pl.multiple_of(2 * step, 2)
            place = pl.ds(pl.multiple_of(16 * step, 16), 16)
            here = mbuf[x, pl.ds(first, 2)].astype(F32)
            after_x = mbuf[x + 1, pl.ds(first, 2)].astype(F32)
            after_y = pltpu.roll(here, CY - 1, 1)
            after_y = jnp.where(iota(here.shape, 1) == CY - 1, 0.0, after_y)
            after_z = pltpu.roll(here, CZ - 1, 2)
            after_z = jnp.where(iota(here.shape, 2) == CZ - 1, 0.0, after_z)
            half = weight[x][None] * here - after_x - after_y - after_z
            for block in range(8):
                lanes = slice(block * CZ, (block + 1) * CZ)
                left[place, lanes] = rows_of(half, block)
                right[place, lanes] = rows_of(here, block)
            return inner

        lax.fori_loop(0, K // 2, pair, 0)
        product = dot_nt(left[...], right[...])
        acc[...] += product[:ROWS]
        zrows[x] = product[ROWS : ROWS + 16]
        pick_row = iota((K, ROWS), 0) * 8
        pick_low = (iota((K, ROWS), 1) == pick_row).astype(F32).astype(BF16)
        pick_high = (iota((K, ROWS), 1) == pick_row + 7).astype(F32).astype(BF16)
        ylow[x] = dot_nn(pick_low, right[:, 0:CZ]).astype(BF16)
        yhigh[x] = dot_nn(pick_high, right[:, 7 * CZ : 8 * CZ]).astype(BF16)
        return carry

    for load in loads:
        load.wait()
    lax.fori_loop(0, CX, plane, 0)

    zhigh[...] = zrows[:, 8:16, :].reshape(K, ROWS).astype(BF16)
    yface = remote(yhigh, yrecv, face_send_sem.at[2], face_recv_sem.at[2], {"mcol": j_next})
    zface = remote(zhigh, zrecv, face_send_sem.at[3], face_recv_sem.at[3], {"mrow": i_next})
    yface.start()
    zface.start()

    xface_up.wait()
    xface_down.wait()

    def stage(step, inner):
        first = pl.multiple_of(2 * step, 2)
        place = pl.ds(pl.multiple_of(16 * step, 16), 16)
        sources = (
            (mbuf[0, pl.ds(first, 2), 0 : CY // 2, :], xrecv_low[pl.ds(first, 2)]),
            (mbuf[CX - 1, pl.ds(first, 2), CY // 2 : CY, :], xrecv_high[pl.ds(first, 2)]),
        )
        for part, (mine, theirs) in enumerate(sources):
            mine = mine.astype(F32)
            theirs = theirs.astype(F32)
            for block in range(4):
                lanes = slice((4 * part + block) * CZ, (4 * part + block + 1) * CZ)
                right[place, lanes] = rows_of(mine, block)
                left[place, lanes] = rows_of(theirs, block)
        return inner

    lax.fori_loop(0, K // 2, stage, 0)
    low_part = fold(dot_nt(left[0:ROWS, 0 : 4 * CZ], right[:, 0 : 4 * CZ]))
    high_part = fold(dot_nt(right[:, 4 * CZ : 8 * CZ], left[0:ROWS, 4 * CZ : 8 * CZ]))
    part_send[0, :, 0:K] = low_part
    part_send[1, :, 0:K] = high_part.T
    parts = [
        remote(
            part_send.at[slot],
            part_recv.at[slot],
            part_send_sem.at[slot],
            part_recv_sem.at[slot],
            target,
        )
        for slot, target in enumerate(
            ({"sub": s_prev}, {"sub": s_next}, {"mcol": j_prev}, {"mrow": i_prev})
        )
    ]
    parts[0].start()
    parts[1].start()

    gram = fold(acc[...])

    yface.wait()
    y_part = jnp.zeros((K, K), F32)
    for x in range(CX):
        y_part = y_part + dot_nt(yrecv[x], ylow[x])
    part_send[2, :, 0:K] = y_part
    parts[2].start()
    zface.wait()
    z_low = zrows[:, 0:8, :].reshape(K, ROWS).astype(BF16)
    z_part = fold(dot_tn(zrecv[...].astype(F32), z_low.astype(F32)))
    part_send[3, :, 0:K] = z_part
    parts[3].start()

    for mask in masks:
        mask.wait()
    for part in parts:
        part.wait()

    own_row = (iota((K, K), 0) < live).astype(F32)
    own_col = mask_own[0:1, 0:K]
    diag = (iota((K, K), 0) == iota((K, K), 1)).astype(F32)
    diagonal = (gram + gram.T) * own_row * own_col + diag * (1.0 - own_row)

    def finish(block, slot, present):
        kept = own_row * mask_recv[slot, 0:1, 0:K]
        return -block * (kept * jnp.where(present, 1.0, 0.0))

    x_low = finish(low_part.T + part_recv[1, :, 0:K], 0, sub > 0)
    x_high = finish(high_part + part_recv[0, :, 0:K], 1, sub < SUB - 1)
    y_low = finish(y_part.T, 2, mcol > 0)
    y_high = finish(part_recv[2, :, 0:K], 3, mcol < mcols - 1)
    z_lower = finish(z_part.T, 4, mrow > 0)
    z_high = finish(part_recv[3, :, 0:K], 5, mrow < mrows - 1)
    own_out[...] = jnp.concatenate(
        [diagonal, x_high, y_high, z_high, x_low, y_low, z_lower, jnp.zeros((K, K), F32)], axis=1
    )

    head = (mrow == 0) & (mcol == 0)
    second = (mrow == 0) & (mcol == 1)
    third = (mrow == 1) & (mcol == 0)

    @pl.when(head)
    def _():
        gathered[sub] = own_out[:, 0 : 4 * K]

    def cross(which, target):
        return remote(
            gathered.at[sub],
            gathered.at[sub],
            cross_send_sem.at[which],
            line_recv_sem.at[0],
            target,
        )

    def line(step):
        return remote(
            gathered.at[sub],
            gathered.at[sub],
            line_send_sem.at[step],
            line_recv_sem.at[step],
            {"sub": lax.rem(sub + step, SUB)},
        )

    def arrival(step):
        source = lax.rem(sub + SUB - step, SUB)
        return remote(
            gathered.at[source],
            gathered.at[source],
            line_send_sem.at[step],
            line_recv_sem.at[step],
            {"sub": source},
        )

    @pl.when(head)
    def _():
        cross(0, {"mcol": j_next}).start()
        cross(1, {"mrow": i_next}).start()

    @pl.when(second | third)
    def _():
        remote(
            gathered.at[sub],
            gathered.at[sub],
            cross_send_sem.at[0],
            line_recv_sem.at[0],
            {"mcol": j_prev},
        ).wait_recv()

    @pl.when(head | second | third)
    def _():
        for step in range(1, SUB):
            line(step).start()
        for step in range(1, SUB):
            arrival(step).wait_recv()
        for step in range(1, SUB):
            line(step).wait_send()

    @pl.when(head)
    def _():
        cross(0, {"mcol": j_next}).wait_send()
        cross(1, {"mrow": i_next}).wait_send()


def factor_kernel(own, gathered, out, rows, xin, xall):
    mrow = lax.axis_index("mrow")
    mcol = lax.axis_index("mcol")
    sub = lax.axis_index("sub")
    mrows = lax.axis_size("mrow")
    mcols = lax.axis_size("mcol")
    position = (mrow * mcols + mcol) * SUB + sub
    head = (mrow == 0) & (mcol == 0)
    second = (mrow == 0) & (mcol == 1)
    third = (mrow == 1) & (mcol == 0)
    odd = lax.rem(sub, 2) == 1

    out[...] = jnp.zeros_like(out)

    def tile(index):
        return pl.ds(pl.multiple_of(index * 128, 128), 128)

    def block(index):
        return own[:, index * K : (index + 1) * K]

    empty = jnp.zeros((K, K), F32)

    @pl.when(jnp.logical_not(head))
    def _():
        diagonal, x_high, y_high, z_high, x_low, y_low, z_low = (block(n) for n in range(7))
        here = position // 2
        pair_even = jnp.concatenate([diagonal, x_high], axis=1)
        pair_odd = jnp.concatenate([x_low, diagonal], axis=1)
        out[:, tile(here)] = jnp.where(odd, pair_odd, pair_even)

        @pl.when(odd & (sub < SUB - 1))
        def _():
            out[:, tile(here + 1)] = jnp.concatenate([x_high, empty], axis=1)

        @pl.when(jnp.logical_not(odd) & (sub > 0))
        def _():
            out[:, tile(here - 1)] = jnp.concatenate([empty, x_low], axis=1)

        def either(value):
            return jnp.where(
                odd,
                jnp.concatenate([empty, value], axis=1),
                jnp.concatenate([value, empty], axis=1),
            )

        for value, present, stride in (
            (y_high, mcol < mcols - 1, SUB // 2),
            (y_low, (mcol > 0) & jnp.logical_not(second), -(SUB // 2)),
            (z_high, mrow < mrows - 1, mcols * SUB // 2),
            (z_low, (mrow > 0) & jnp.logical_not(third), -(mcols * SUB // 2)),
        ):

            @pl.when(present)
            def _():
                out[:, tile(here + stride)] = either(value)

    @pl.when(head | second | third)
    def _():
        lane = iota((K, 8 * K), 1) >> 6

        def placed(index):
            values = gathered[index]
            first = jnp.concatenate([values[:, 2 * K : 3 * K]] * 8, axis=1)
            other = jnp.concatenate([values[:, 3 * K : 4 * K]] * 8, axis=1)
            first = jnp.where(lane == index, first, 0.0)
            other = jnp.where(lane == index, other, 0.0)
            return jnp.concatenate([first, other], axis=1)

        xin[...] = placed(0)

        def step(index, pivot):
            state = jnp.concatenate([pivot, gathered[index][:, K : 2 * K]], axis=1)
            inverse = (iota((K, 128), 0) == iota((K, 128), 1)).astype(F32)
            row_ids = iota((K, 1), 0)
            for col in range(K):
                top = (col // 8) * 8
                scale = lax.rsqrt(state[col : col + 1, col : col + 1])
                line = state[col : col + 1, :] * scale
                line_inverse = inverse[col : col + 1, :] * scale
                rows[index, col : col + 1, 0:128] = line
                rows[index, col : col + 1, 128:256] = line_inverse
                factor = state[:, col : col + 1] * scale
                factor = jnp.where(row_ids > col, factor, 0.0)
                state = state - factor * line
                inverse = inverse - factor * line_inverse
            coupled = rows[index, :, K : 2 * K]
            solved = dot_nn(rows[index, :, 2 * K : 3 * K], xin[...], HI)
            xall[pl.ds(pl.multiple_of(index * K, K), K), :] = solved
            following = jnp.minimum(index + 1, SUB - 1)
            xin[...] = placed(following) - dot_tn(coupled, solved, HI)
            return gathered[following][:, 0:K] - dot_tn(coupled, coupled, HI)

        lax.fori_loop(0, SUB, step, gathered[0][:, 0:K])

    @pl.when(head)
    def _():
        upper = iota((K, K), 0) <= iota((K, K), 1)
        mine = jnp.where(upper, rows[sub, :, 0:K], 0.0).T
        before = rows[jnp.maximum(sub - 1, 0), :, K : 2 * K].T
        here = sub // 2
        out[:, tile(here)] = jnp.where(
            odd,
            jnp.concatenate([before, mine], axis=1),
            jnp.concatenate([mine, empty], axis=1),
        )

        @pl.when(jnp.logical_not(odd) & (sub > 0))
        def _():
            out[:, tile(here - 1)] = jnp.concatenate([empty, before], axis=1)

    @pl.when(second | third)
    def _():
        which = jnp.where(third, SUB, 0) + sub
        mine = xall[:, tile(which // 2)]
        mine = jnp.where(odd, pltpu.roll(mine, K, 1), mine)
        out[:, 0 : 8 * K] = mine.T[0:K, :]
        product = dot_tn(mine, xall[...], HI)[0:K]
        out[:, 8 * K : 16 * K] -= product[:, 0 : 8 * K]
        far = mcols * SUB * K
        out[:, far : far + 8 * K] -= product[:, 8 * K : 16 * K]


def shards(deflation, reaction, vector_counts):
    vmem = pl.BlockSpec(memory_space=pltpu.VMEM)
    own, gathered = pl.pallas_call(
        assemble_kernel,
        out_shape=(
            jax.ShapeDtypeStruct((K, 8 * K), F32),
            jax.ShapeDtypeStruct((SUB, K, 4 * K), F32),
        ),
        in_specs=[
            pl.BlockSpec(memory_space=pl.ANY),
            vmem,
            pl.BlockSpec(memory_space=pltpu.SMEM),
        ],
        out_specs=(vmem, vmem),
        scratch_shapes=[
            pltpu.VMEM((CX + 1, K, CY, CZ), BF16),
            pltpu.VMEM((ROWS + 16, 8 * CZ), BF16),
            pltpu.VMEM((ROWS, 8 * CZ), BF16),
            pltpu.VMEM((ROWS, ROWS), F32),
            pltpu.VMEM((CX, CY, CZ), F32),
            pltpu.VMEM((CX, 16, ROWS), F32),
            pltpu.VMEM((CX, K, CZ), BF16),
            pltpu.VMEM((CX, K, CZ), BF16),
            pltpu.VMEM((CX, K, CZ), BF16),
            pltpu.VMEM((K, ROWS), BF16),
            pltpu.VMEM((K, ROWS), BF16),
            pltpu.VMEM((K, CY // 2, CZ), BF16),
            pltpu.VMEM((K, CY // 2, CZ), BF16),
            pltpu.VMEM((8, 128), F32),
            pltpu.VMEM((6, 8, 128), F32),
            pltpu.VMEM((4, K, 128), F32),
            pltpu.VMEM((4, K, 128), F32),
            pltpu.SemaphoreType.DMA((CX,)),
            pltpu.SemaphoreType.DMA((6,)),
            pltpu.SemaphoreType.DMA((6,)),
            pltpu.SemaphoreType.DMA((4,)),
            pltpu.SemaphoreType.DMA((4,)),
            pltpu.SemaphoreType.DMA((4,)),
            pltpu.SemaphoreType.DMA((4,)),
            pltpu.SemaphoreType.DMA((SUB,)),
            pltpu.SemaphoreType.DMA((2,)),
            pltpu.SemaphoreType.DMA((SUB,)),
        ],
        compiler_params=pltpu.CompilerParams(
            collective_id=0, has_side_effects=True, vmem_limit_bytes=56 * 1024 * 1024
        ),
        name="assemble",
    )(deflation, reaction, vector_counts)
    return pl.pallas_call(
        factor_kernel,
        out_shape=jax.ShapeDtypeStruct((K, 128 * K), F32),
        in_specs=[vmem, vmem],
        out_specs=vmem,
        scratch_shapes=[
            pltpu.VMEM((SUB, K, 256), F32),
            pltpu.VMEM((K, 16 * K), F32),
            pltpu.VMEM((SUB * K, 16 * K), F32),
        ],
        compiler_params=pltpu.CompilerParams(vmem_limit_bytes=56 * 1024 * 1024),
        name="factor",
    )(own, gathered)


def solution(mesh):
    return jax.shard_map(
        shards,
        mesh=mesh,
        in_specs=(
            P(None, "sub", "mcol", "mrow"),
            P("sub", "mcol", "mrow"),
            P(("mrow", "mcol", "sub")),
        ),
        out_specs=P(("mrow", "mcol", "sub"), None),
        check_vma=False,
    )
```

time: 696 us -> 122 us (0.18); the launches traced: 687 us -> 121 us
  waiting for transfers between devices: 326 us -> 0 us
  other arithmetic: 186 us -> 0 us
  Pallas kernels: 0 us -> 120 us
  local copies, waits for them, and re-layouts: 108 us -> 0 us
  matrix products: 33.3 us -> 0 us
  between operations: 17.6 us -> 0.66 us
  starting transfers between devices: 15.9 us -> 0 us
    psum x2 -> x0, waiting for transfers between devices: 316 us -> none  [shards(): compact = lax.psum(contribution, ('mrow', 'mcol', 'sub'))]
    pallas_call x0 -> x2, Pallas kernels: none -> 120 us  [the longest x1 69 us: shards(): pl.pallas_call(assemble_kernel, out_shape=(jax.ShapeDtypeStruct((K, 8 * K...]
    another operation x18 -> x0, other arithmetic: 108 us -> none  [the longest x13 68.6 us: shards(): pivot_factor = jnp.linalg.cholesky(stacked[pivot_start:pivot_start + PANEL])]
    dot_general x1 -> x0, other arithmetic: 45.1 us -> none  [inner_products(): lax.dot_general(left_side.reshape(vectors, -1), right_side.reshape(vector...]
    slice x8 -> x0, local copies, waits for them, and re-layouts: 33.9 us -> none  [the longest x2 18 us: padded_2(): lax.slice_in_dim(cells, cells.shape[dim] - width, cells.shape[dim], axis=...]
    another operation x22 -> x0, local copies, waits for them, and re-layouts: 29.6 us -> none
    dot_general x9 -> x0, matrix products: 25.8 us -> none  [the longest x7 22.7 us: inner_products(): lax.dot_general(left_side.reshape(vectors, -1), right_side.reshape(vector...]
    scatter x3 -> x0, local copies, waits for them, and re-layouts: 18.8 us -> none  [shards(): jnp.zeros((vectors, order_total), jnp.float32).at[:, jnp.asarray(row_ids)]]
  transfers between devices with their start and end apart: 8 -> 0, of which waited for: 4 -> 0; matrix products, arithmetic and copies ran while one was open for 15% -> 0% of each run, Pallas kernels for 0% -> 0%
where the time goes in v1:
time: 122 us; the launch traced here: 121 us
  Pallas kernels  120 us (98%)
    pallas_call x1, Pallas kernels, shards(): pl.pallas_call(assemble_kernel, out_shape=(jax.ShapeDtypeStruct((K, 8 * K...  69 us
    pallas_call x1, Pallas kernels, shards(): pl.pallas_call(factor_kernel, out_shape=jax.ShapeDtypeStruct((K, 128 * K)...  51 us

profile of v1, /device:TPU:2, one launch (start us, length us, event | category | flops | bytes accessed | tf_op | source)
XLA Modules:
  0.0 120.7 jit_solution(5859681810648330791)
XLA Ops:
  0.7 69.0 %assemble.1 = (f32[64,512]{1,0:T(8,128)}, f32[8,64,256]{2,1,0:T(8,128)}) custom-call(bf16[64,8,64,256]{3,2,1,0:T(8,128)(2,1)} %defl.1, f32[8,64,256]{2,1,0:T(8,128)} %react.1, s32[1]{0:T(128)S(6)} %copy.4.count), custom_call_target="tpu_custom_call" | custom-call | tf_op jit(solution)/shard_map/assemble/pallas_call | solution.py:484
  69.7 51.0 %factor.1 = f32[64,8192]{1,0:T(8,128)} custom-call(f32[64,512]{1,0:T(8,128)} %get-tuple-element.7.own, f32[8,64,256]{2,1,0:T(8,128)} %get-tuple-element.8.gathered), custom_call_target="tpu_custom_call" | custom-call | tf_op jit(solution)/shard_map/factor/pallas_call | solution.py:530
